TPU v7x, 256 devices: a whole 4x4x8 slice. The times are simulated.
256 devices in a mesh: row: 16 (over y, x), col: 16 (over z, core).
Axes of the slice: x: 4, y: 4, z: 8, core: 2. Of those that a mesh axis runs over, the one named last changes fastest.
Arguments:
- amplitudes: float32 [512, 576, 576], P('row', None, 'col'), may hold values from -6 to 6
- integrals: float32 [576, 576, 3, 576], P('row', 'col'), may hold values from -0.03125 to 0.03125
- virt_irrep: int32 [576], replicated, may hold values from 0 to 7
- occ_irrep: int32 [60], replicated, may hold values from 0 to 7
- pair_index: int32 [512, 2], replicated, may hold values from 0 to 59
Outputs:
- ladder: float32 [512, 3, 576], P('row', None, 'col')
Inputs may be any that keep to these rules, and one draw needn't show every extreme that they name: `virt_irrep`: irrep labels of the virtual orbitals, in no particular order. `pair_index`: indices of occupied orbitals; pairs may repeat.
All inputs are finite; a program needn't handle non-finite values.
Results may differ from a plain program's by a relative error of at most 0.00011.
Values sent between devices are 32-bit elements; how exact they have to be, the bound alone decides.
No kernel may reach another device: no remote copies, remote signals or barrier semaphores. Data moves between devices by JAX's collectives and lax.ppermute only.
A program may use at most 128 MiB of HBM per device.

v0:
```python
import jax
import jax.numpy as jnp
from jax import lax
from jax.sharding import PartitionSpec as P


def pair_labels(occ_irrep, pair_index):
    orbits = jnp.arange(occ_irrep.shape[0], dtype=jnp.int32)
    onehot = (pair_index[:, :, None] == orbits[None, None, :]).astype(jnp.int32)
    labels = jnp.sum(onehot * occ_irrep[None, None, :], axis=2)
    return jnp.bitwise_xor(labels[:, 0], labels[:, 1])


def per_device(amplitudes, integrals, virt_irrep, occ_irrep, pair_index):
    n_col = lax.axis_size("col")
    row_at = lax.axis_index("row")
    col_at = lax.axis_index("col")
    c_rows = integrals.shape[0]
    d_cols = integrals.shape[1]
    slab = integrals.shape[2]
    n_virt = integrals.shape[3]
    pair_dev = amplitudes.shape[0]
    b_cols = n_virt // n_col
    exchanged = lax.all_to_all(amplitudes, "row", split_axis=1, concat_axis=0, tiled=True)
    pair_count = exchanged.shape[0]
    pair_sym = pair_labels(occ_irrep, pair_index)
    labels_c = lax.dynamic_slice_in_dim(virt_irrep, row_at * c_rows, c_rows)
    labels_d = lax.dynamic_slice_in_dim(virt_irrep, col_at * d_cols, d_cols)
    cd_sym = jnp.bitwise_xor(labels_c[:, None], labels_d[None, :])
    amp_sym = jnp.where(cd_sym[None, :, :] == pair_sym[:, None, None], exchanged, jnp.float32(0.0))
    partials = jnp.dot(
        amp_sym.reshape(pair_count, c_rows * d_cols),
        integrals.reshape(c_rows * d_cols, slab * n_virt),
        precision=lax.Precision.HIGHEST,
        preferred_element_type=jnp.float32,
    )
    partials = partials.reshape(pair_count, slab, n_virt)
    by_block = lax.psum_scatter(partials, "col", scatter_dimension=2, tiled=True)
    summed = lax.psum_scatter(by_block, "row", scatter_dimension=0, tiled=True)
    local_sym = lax.dynamic_slice_in_dim(pair_sym, row_at * pair_dev, pair_dev)
    labels_b = lax.dynamic_slice_in_dim(virt_irrep, col_at * b_cols, b_cols)
    ab_sym = jnp.bitwise_xor(virt_irrep[:slab][:, None], labels_b[None, :])
    keep = ab_sym[None, :, :] == local_sym[:, None, None]
    return jnp.where(keep, summed, jnp.float32(0.0))


def solution(mesh):
    return jax.shard_map(
        per_device,
        mesh=mesh,
        in_specs=(P("row", None, "col"), P("row", "col", None, None), P(), P(), P()),
        out_specs=P("row", None, "col"),
        check_vma=False,
    )
```

profile of v0, /device:TPU:2, one launch (start us, length us, event | category | flops | bytes accessed | tf_op | source)
XLA Modules:
  0.0 365.5 jit_solution(1993708538343620225)
XLA Ops:
  6.5 7.2 %copy.32 = f32[32,576,36]{2,0,1:T(8,128)} copy(f32[32,576,36]{1,0,2:T(8,128)} %param.5) | data formatting | bytes 5308416 | tf_op args[0]
  13.8 0.0 copy-start
  13.8 0.0 copy-start.1
  13.8 13.2 %reshape.105 = f32[16,1,41472]{2,1,0:T(1,128)} reshape(f32[576,32,36]{2,1,0:T(8,128)} %bitcast.25) | data formatting | bytes 5308416
  27.0 7.5 %all-to-all-start = ((f32[16,1,41472]{2,1,0:T(1,128)}), f32[16,1,41472]{2,1,0:T(1,128)S(1)}, u32[]{:S(2)}, u32[]{:S(2)}) async-start(f32[16,1,41472]{2,1,0:T(1,128)} %reshape.105), calls=%async_computation | async-start | bytes 5308416 | tf_op jit(solution)/shard_map/all_to_all | solution.py:24
  34.4 0.2 all-reduce.3.cloned.1.call-start
  34.7 0.0 copy-done
  34.7 0.0 copy-done.1
  34.7 0.2 fusion
  34.9 0.5 broadcast.61
  35.4 0.7 fusion.1
  36.1 0.1 xor.52
  36.2 13.5 %copy.34 = f32[36,36,3,576]{3,2,1,0:T(4,128)} copy(f32[36,36,3,576]{3,1,2,0:T(8,128)} %param.6) | data formatting | bytes 17915904 | tf_op args[1]
  49.7 16.2 %reshape.87 = f32[1296,1728]{1,0:T(8,128)} reshape(f32[36,36,3,576]{3,2,1,0:T(4,128)} %copy.34) | data formatting | bytes 17915904 | tf_op jit(solution)/shard_map/reshape | solution.py:33
  65.9 0.0 copy-start.2
  65.9 11.1 %copy.35 = f32[1728,1296]{1,0:T(8,128)} copy(f32[1728,1296]{0,1:T(8,128)} %bitcast.26) | data formatting | bytes 17915904 | tf_op jit(solution)/shard_map/dot_general | solution.py:31
  76.9 0.0 copy-done.2
  76.9 0.1 fusion.2
  77.0 0.1 broadcast_xor_fusion
  77.1 0.0 all-to-all-done
  77.1 0.5 broadcast.62
  77.6 9.1 %reduce.5 = f32[16,41472]{1,0:T(8,128)} reduce(f32[16,1,41472]{2,1,0:T(1,128)S(1)} %all-to-all-done, f32[]{:T(128)} %broadcast.62), dimensions={1}, to_apply=%all_to_all.11.reduce_sub_computation | reduce | bytes 5308420 | tf_op jit(solution)/shard_map/all_to_all | solution.py:24
  86.8 19.1 %reshape.106 = f32[576,32,36]{2,1,0:T(8,128)} reshape(f32[16,41472]{1,0:T(8,128)} %reduce.5) | data formatting | bytes 5308416
  105.9 11.8 %copy.33 = f32[32,16,36,36]{0,1,3,2:T(8,128)} copy(f32[32,16,36,36]{3,0,2,1:T(8,128)} %bitcast.24) | data formatting | bytes 5308416 | tf_op jit(solution)/shard_map/all_to_all | solution.py:24
  117.7 8.7 %bitcast_select_fusion = f32[16,32,36,36]{1,0,3,2:T(8,128)} fusion(f32[32,16,36,36]{0,1,3,2:T(8,128)} %copy.33, s32[16,32]{1,0:T(8,128)S(1)} %xor.52, s32[36,36]{1,0:T(8,128)S(1)} %broadcast_xor_fusion), kind=kLoop, calls=%fused_computation | loop fusion | flops 1327104 | bytes 5315648 | tf_op jit(solution)/shard_map/jit(_where)/select_n | solution.py:30
  126.4 7.6 %reshape.88 = f32[512,1296,1]{0,1,2:T(8,128)S(1)} reshape(f32[16,32,36,36]{1,0,3,2:T(8,128)} %bitcast_select_fusion) | data formatting | bytes 5308416 | tf_op jit(solution)/shard_map/jit(_where)/select_n | solution.py:30
  134.0 0.0 copy-start.3
  134.0 0.0 slice-start
  134.0 20.2 %fusion.3 = f32[512,3,576]{0,2,1:T(8,128)} fusion(f32[512,1296,1]{0,1,2:T(8,128)S(1)} %reshape.88, f32[3,576,1296]{2,1,0:T(8,128)} %bitcast.27), kind=kOutput, calls=%fused_computation.11 | convolution fusion | flops 13759414272 | bytes 15151104 | tf_op jit(solution)/shard_map/dot_general | solution.py:31
  154.2 0.0 all-reduce.3.cloned.1.call-update
  154.2 0.0 reduce-scatter.5.cloned.1.call-start
  154.3 0.0 copy-done.3
  154.3 0.6 dynamic-slice.1
  155.5 121.2 %all-reduce.3.cloned.1.call-done = f32[512,3,576]{0,2,1:T(8,128)} async-done(((f32[512,3,576]{0,2,1:T(8,128)}), f32[512,3,576]{0,2,1:T(8,128)}) %all-reduce.3.cloned.1.call-update) | async-done | bytes 3538960
  276.7 1.0 constant_dynamic-slice_fusion
  277.8 0.8 copy.41
  278.6 0.0 reduce-scatter.5.cloned.1.call-update
  278.6 0.1 dynamic-slice_bitcast_fusion
  278.7 0.0 slice-done
  278.7 0.1 broadcast_xor_fusion.1
  278.8 78.2 %reduce-scatter.5.cloned.1.call-done = f32[32,108]{1,0:T(8,128)} async-done(((f32[512,108]{1,0:T(8,128)}), f32[32,108]{1,0:T(8,128)}) %reduce-scatter.5.cloned.1.call-update) | async-done | bytes 13840
  357.0 0.8 reshape.93
  357.8 0.1 copy.40
  357.9 0.1 compare_select_fusion.1
  358.0 0.7 copy.36
  (1 shorter events, 0.0 us)
Async XLA Ops:
  13.8 20.9 %copy-start = (s32[512,2]{0,1:T(2,128)S(1)}, s32[512,2]{0,1:T(2,128)}, u32[]{:S(2)}) copy-start(s32[512,2]{0,1:T(2,128)} %param.9) | copy-start | bytes 12292
  13.8 20.9 %copy-start.1 = (s32[60]{0:T(128)S(1)}, s32[60]{0:T(128)}, u32[]{:S(2)}) copy-start(s32[60]{0:T(128)} %param.8) | copy-start | bytes 724
  27.0 50.1 %all-to-all-start = ((f32[16,1,41472]{2,1,0:T(1,128)}), f32[16,1,41472]{2,1,0:T(1,128)S(1)}, u32[]{:S(2)}, u32[]{:S(2)}) async-start(f32[16,1,41472]{2,1,0:T(1,128)} %reshape.105), calls=%async_computation | async-start | bytes 5308416 | tf_op jit(solution)/shard_map/all_to_all | solution.py:24
  34.4 242.3 %all-reduce.3.cloned.1.call-start = ((), (), s32[]{:S(2)}) async-start(), calls=%async_computation.3 | async-start | bytes 7077888
  65.9 11.1 %copy-start.2 = (s32[576]{0:T(1024)S(1)}, s32[576]{0:T(1024)}, u32[]{:S(2)}) copy-start(s32[576]{0:T(1024)} %param.7) | copy-start | bytes 6916
  134.0 20.3 %copy-start.3 = (u32[256]{0:T(256)S(1)}, u32[256]{0:T(256)}, u32[]{:S(2)}) copy-start(u32[256]{0:T(256)} %constant.25) | copy-start | bytes 3076
  134.0 144.7 %slice-start = ((s32[576]{0:T(1024)}), s32[3]{0:T(128)S(1)}, s32[]{:S(2)}) async-start(s32[576]{0:T(1024)} %param.7), calls=%async_computation.4 | async-start | bytes 1024 | tf_op jit(solution)/shard_map/slice | solution.py:42
  154.2 202.7 %reduce-scatter.5.cloned.1.call-start = ((), (), s32[]{:S(2)}) async-start(), calls=%async_computation.2 | async-start | bytes 278528
Sparse Core Ops, SparseCore 0:
  154.4 122.3 all-reduce.2
  280.2 76.7 reduce-scatter.4
where the time goes:
time: 367 us; the launch traced here: 366 us
  waiting for transfers between devices  199 us (54%)
  local copies, waits for them, and re-layouts  105 us (29%)
  matrix products  20.2 us (6%)
  other arithmetic  19 us (5%)
  between operations  14.2 us (4%)
  starting transfers between devices  7.74 us (2%)
    unnamed x4, waiting for transfers between devices  199 us
    unnamed x18, local copies, waits for them, and re-layouts  56.4 us
    dot_general x1, matrix products, per_device(): jnp.dot(amp_sym.reshape(pair_count, c_rows * d_cols), integrals.reshape(c...  20.2 us
    reshape x1, local copies, waits for them, and re-layouts, per_device(): integrals.reshape(c_rows * d_cols, slab * n_virt)  16.2 us
    all_to_all x2, local copies, waits for them, and re-layouts, per_device(): lax.all_to_all(amplitudes, 'row', split_axis=1, concat_axis=0, tiled=True)  12.3 us
    dot_general x1, local copies, waits for them, and re-layouts, per_device(): jnp.dot(amp_sym.reshape(pair_count, c_rows * d_cols), integrals.reshape(c...  11.1 us
    all_to_all x1, other arithmetic, per_device(): lax.all_to_all(amplitudes, 'row', split_axis=1, concat_axis=0, tiled=True)  9.14 us
    select_n x1, other arithmetic, per_device(): jnp.where(cd_sym[None, :, :] == pair_sym[:, None, None], exchanged, jnp.f...  8.72 us
  transfers between devices with their start and end apart: 3, of which 2 were waited for; matrix products, arithmetic and copies ran while one was open for 12% of the time, Pallas kernels for 0%

commit v1 on v0

v1 whole, which is shorter than its diff:
```python
import functools

import jax
import jax.numpy as jnp
from jax import lax
from jax.experimental import pallas as pl
from jax.experimental.pallas import tpu as pltpu
from jax.sharding import Mesh, PartitionSpec as P

F32 = jnp.float32
BF16 = jnp.bfloat16
I32 = jnp.int32

C = 36
D = 36
PD = 32
NY = NX = 4
NR = NY * NX
NZ = 8
SLAB = 3
NV = 576
PAIRS = 512
NO = 60
CP = 40
K = D * CP
KP = 1536
FITS = ((6, 1), (6, 2), (9, 3))

SMEM = pl.BlockSpec(memory_space=pltpu.SMEM)
VMEM = pl.BlockSpec(memory_space=pltpu.VMEM)
HBM = pl.BlockSpec(memory_space=pltpu.HBM)


def rows_of(slots):
    return -(-slots * 36 // 8) * 8


def in_hbm(x):
    return pltpu.with_memory_space_constraint(x, pltpu.HBM)


def labels_kernel(occ_ref, virt_ref, pairs_ref, row_ref, sym_ref, slot_ref, which_ref):
    pairs = pairs_ref[...]
    found = jnp.zeros_like(pairs)
    for o in range(NO):
        found = jnp.where(pairs == o, occ_ref[o], found)
    sym_ref[...] = jnp.bitwise_xor(found[0:1], found[1:2])

    labels = row_ref[...]
    at = lax.rem(lax.broadcasted_iota(I32, labels.shape, 1), D)
    place = jnp.zeros_like(labels)
    for k in range(1, D):
        same = (pltpu.roll(labels, k, 1) == labels) & (at >= k)
        place = place + same.astype(I32)
    top = jnp.max(place)
    deep = jnp.maximum(slab_slot(virt_ref, jnp.int32(1)), slab_slot(virt_ref, jnp.int32(2)))
    which = jnp.int32(len(FITS) - 1)
    for i, (tiles, slots) in reversed(list(enumerate(FITS[:-1]))):
        which = jnp.where((top < 4 * tiles) & (deep < slots), i, which)
    which_ref[0] = which
    slot_ref[...] = jnp.where(which < len(FITS) - 1, place, at)


def slab_slot(virt_ref, a):
    first = (a > 0) & (virt_ref[0] == virt_ref[a])
    second = (a > 1) & (virt_ref[1] == virt_ref[a])
    return first.astype(I32) + second.astype(I32)


def label_all(occ_irrep, virt_irrep, pairs, virt_row):
    return pl.pallas_call(
        labels_kernel,
        out_shape=[
            jax.ShapeDtypeStruct((1, PAIRS), I32),
            jax.ShapeDtypeStruct((1, NV), I32),
            jax.ShapeDtypeStruct((1,), I32),
        ],
        in_specs=[SMEM, SMEM, VMEM, VMEM],
        out_specs=[VMEM, VMEM, SMEM],
        name="label_all",
    )(occ_irrep, virt_irrep, pairs, virt_row)


def pack_kernel(tiles, at_ref, virt_ref, slot_ref, x_hbm, cl_ref, sym_ref, o_hbm, x_buf, f_buf, t_buf, o_buf, in_sems, out_sems):
    def fetch(q):
        return pltpu.make_async_copy(x_hbm.at[pl.ds(4 * q, 4)], x_buf.at[pl.ds(4 * q, 4)], in_sems.at[q])

    for q in range(D // 4):
        fetch(q).start()
    f_buf[...] = jnp.zeros_like(f_buf)
    pair = at_ref[0] * PD + lax.broadcasted_iota(I32, (PD, PAIRS), 0)
    mine = lax.broadcasted_iota(I32, (PD, PAIRS), 1) == pair
    sym = jnp.sum(jnp.where(mine, sym_ref[...], 0), axis=1, keepdims=True)
    first = at_ref[1] * D

    @pl.loop(0, D // 4)
    def _(q):
        fetch(q).wait()
        for i in range(4):
            d = 4 * q + i
            keep = jnp.bitwise_xor(cl_ref[...], virt_ref[first + d]) == sym
            at = slot_ref[0, first + d]
            f_buf[at] = f_buf[at] + jnp.where(keep, x_buf[d], 0.0)

    for q in range(tiles):
        t_buf[q % 2] = f_buf[4 * q:4 * q + 4].reshape(4 * PD, NV).T
        for r in range(NR):
            o_buf[r, q * C:(q + 1) * C, :] = t_buf[q % 2, r * C:(r + 1) * C, :]
    out = []
    for r in range(NR):
        copy = pltpu.make_async_copy(o_buf.at[r], o_hbm.at[r], out_sems.at[r])
        copy.start()
        out.append(copy)
    for copy in out:
        copy.wait()


def pack_amplitudes(tiles, at, virt, slots, amps, cl, sym):
    block = (NR, tiles * C, 128)
    return pl.pallas_call(
        functools.partial(pack_kernel, tiles),
        out_shape=pltpu.HBM(block, F32),
        in_specs=[SMEM, SMEM, SMEM, HBM, VMEM, VMEM],
        out_specs=HBM,
        scratch_shapes=[
            pltpu.VMEM((D, PD, NV), F32),
            pltpu.VMEM((4 * tiles, PD, NV), F32),
            pltpu.VMEM((2, NV, 128), F32),
            pltpu.VMEM(block, F32),
            pltpu.SemaphoreType.DMA((D // 4,)),
            pltpu.SemaphoreType.DMA((NR,)),
        ],
        compiler_params=pltpu.CompilerParams(vmem_limit_bytes=20 << 20),
        name="pack_amplitudes",
    )(at, virt, slots, in_hbm(amps), cl, sym)


STEP = 6


def integrals_kernel(v_hbm, hi_hbm, lo_hbm, v_buf, h_buf, l_buf, in_sems, out_sems):
    def fetch(d, a):
        return pltpu.make_async_copy(v_hbm.at[:, a, d], v_buf.at[d, a], in_sems.at[d, a])

    @pl.loop(0, D)
    def _(d):
        for a in range(SLAB):
            fetch(d, a).start()

    zero = jnp.zeros((CP - C, NV), F32)
    for a in range(SLAB):
        h_buf[a, K:, :] = jnp.zeros((KP - K, NV), BF16)
        l_buf[a, K:, :] = jnp.zeros((KP - K, NV), BF16)
    out = []
    for i in range(D // STEP):
        @pl.loop(i * STEP // 2, (i + 1) * STEP // 2)
        def _(pair):
            d = 2 * pair
            at = pl.multiple_of(pair * 2 * CP, 16)
            for a in range(SLAB):
                fetch(d, a).wait()
                fetch(d + 1, a).wait()
                x = jnp.concatenate([v_buf[d, a], zero, v_buf[d + 1, a], zero], axis=0)
                h = x.astype(BF16)
                h_buf[a, pl.ds(at, 2 * CP), :] = h
                l_buf[a, pl.ds(at, 2 * CP), :] = (x - h.astype(F32)).astype(BF16)

        rows = pl.ds(i * STEP * CP, STEP * CP if (i + 1) * STEP < D else KP - i * STEP * CP)
        for n, (buf, hbm) in enumerate(((h_buf, hi_hbm), (l_buf, lo_hbm))):
            copy = pltpu.make_async_copy(buf.at[:, rows], hbm.at[:, rows], out_sems.at[n, i])
            copy.start()
            out.append(copy)
    for copy in out:
        copy.wait()


def split_integrals(v_t):
    block = (SLAB, KP, NV)
    return pl.pallas_call(
        integrals_kernel,
        out_shape=[pltpu.HBM(block, BF16)] * 2,
        in_specs=[HBM],
        out_specs=[HBM] * 2,
        scratch_shapes=[
            pltpu.VMEM((D, SLAB, C, NV), F32),
            pltpu.VMEM(block, BF16),
            pltpu.VMEM(block, BF16),
            pltpu.SemaphoreType.DMA((D, SLAB)),
            pltpu.SemaphoreType.DMA((2, D // STEP)),
        ],
        compiler_params=pltpu.CompilerParams(vmem_limit_bytes=28 << 20),
        cost_estimate=pl.CostEstimate(flops=20_000_000, bytes_accessed=36_000_000, transcendentals=0),
        name="split_integrals",
    )(in_hbm(v_t))


def regroup(blocks):
    lane = lax.broadcasted_iota(I32, blocks[0].shape, 1) // 32
    out = []
    for i in range(4):
        total = None
        for s in range(4):
            piece = blocks[s] if s == i else pltpu.roll(blocks[s], (32 * (s - i)) % 128, 1)
            total = piece if total is None else jnp.where(lane == s, piece, total)
        out.append(total)
    return out


def tn_dot(x, y):
    return lax.dot_general(x, y, (((0,), (0,)), ((), ())), preferred_element_type=F32)


def products_kernel(slots, at_ref, virt_ref, slot_ref, r_ref, sym_ref, cl_ref, bl_ref, vh_hbm, vl_hbm,
                    own_ref, away_ref, f_buf, h_buf, l_buf, t_buf, vh_ref, vl_ref, sems):
    def fetch(a, n):
        hbm, buf = ((vh_hbm, vh_ref), (vl_hbm, vl_ref))[n]
        return pltpu.make_async_copy(hbm.at[a], buf.at[a], sems.at[a, n])

    for a in range(SLAB):
        for n in range(2):
            fetch(a, n).start()
    first = at_ref[1] * D
    h_buf[K:, :] = jnp.zeros((KP - K, PAIRS), BF16)
    l_buf[K:, :] = jnp.zeros((KP - K, PAIRS), BF16)
    zero = jnp.zeros((CP - C, 128), F32)
    tiles = r_ref.shape[1] // C

    @pl.loop(0, NY)
    def _(y):
        for q in range(tiles):
            blocks = [jnp.concatenate([r_ref[4 * y + s, q * C:(q + 1) * C, :], zero], axis=0) for s in range(4)]
            for i, x in enumerate(regroup(blocks)):
                f_buf[y, 4 * q + i] = x

    @pl.loop(0, D // 2)
    def _(pair):
        d = 2 * pair
        at = pl.multiple_of(pair * 2 * CP, 16)
        for y in range(NY):
            cut = slice(y * 128, (y + 1) * 128)
            labels = jnp.bitwise_xor(cl_ref[...], sym_ref[:, cut])
            parts = [jnp.where(labels == virt_ref[first + e], f_buf[y, slot_ref[0, first + e]], 0.0) for e in (d, d + 1)]
            x = jnp.concatenate(parts, axis=0)
            h = x.astype(BF16)
            h_buf[pl.ds(at, 2 * CP), cut] = h
            l_buf[pl.ds(at, 2 * CP), cut] = (x - h.astype(F32)).astype(BF16)

    if slots < SLAB:
        t_buf[...] = jnp.zeros_like(t_buf)

    @pl.loop(0, SLAB)
    def _(a):
        fetch(a, 0).wait()
        fetch(a, 1).wait()
        out = tn_dot(vh_ref[a], h_buf[...])
        out += tn_dot(vh_ref[a], l_buf[...])
        out += tn_dot(vl_ref[a], h_buf[...])
        if slots < SLAB:
            at = slab_slot(virt_ref, a)
            for y in range(NY):
                cut = slice(y * 128, (y + 1) * 128)
                keep = jnp.bitwise_xor(bl_ref[...], virt_ref[a]) == sym_ref[:, cut]
                t_buf[at, :, cut] = t_buf[at, :, cut] + jnp.where(keep, out[:, cut], 0.0)
        else:
            t_buf[a] = out

    for flag in range(2):
        @pl.when(at_ref[2] == flag)
        def _():
            for j in range(2 * NZ):
                o_ref = own_ref if j % 2 == flag else away_ref
                for t in range(slots):
                    o_ref[j // 2, t * 36:(t + 1) * 36, :] = t_buf[t, j * 36:(j + 1) * 36, :]
    tail = rows_of(slots) - slots * 36
    if tail:
        for z in range(NZ):
            own_ref[z, slots * 36:, :] = jnp.zeros((tail, PAIRS), F32)
            away_ref[z, slots * 36:, :] = jnp.zeros((tail, PAIRS), F32)


def products(slots, at, virt, dslots, recv, sym, cl, bl, vh, vl):
    block = jax.ShapeDtypeStruct((NZ, rows_of(slots), PAIRS), F32)
    folded = recv.shape[1] // C * 4
    return pl.pallas_call(
        functools.partial(products_kernel, slots),
        out_shape=[block, block],
        in_specs=[SMEM] * 3 + [VMEM] * 4 + [HBM] * 2,
        out_specs=[VMEM] * 2,
        scratch_shapes=[
            pltpu.VMEM((NY, folded, CP, 128), F32),
            pltpu.VMEM((KP, PAIRS), BF16),
            pltpu.VMEM((KP, PAIRS), BF16),
            pltpu.VMEM((slots, NV, PAIRS), F32),
            pltpu.VMEM((SLAB, KP, NV), BF16),
            pltpu.VMEM((SLAB, KP, NV), BF16),
            pltpu.SemaphoreType.DMA((SLAB, 2)),
        ],
        compiler_params=pltpu.CompilerParams(vmem_limit_bytes=34 << 20),
        cost_estimate=pl.CostEstimate(flops=2 * 3 * NV * SLAB * KP * PAIRS, bytes_accessed=10_000_000, transcendentals=0),
        name="products",
    )(at, virt, dslots, recv, sym, cl, bl, in_hbm(vh), in_hbm(vl))


def pair_kernel(slots, own_ref, other_ref, o_hbm, o_buf, sems):
    jb = rows_of(slots)

    def put(r):
        return pltpu.make_async_copy(o_buf.at[r], o_hbm.at[r], sems.at[r])

    for y in range(NY):
        cut = slice(y * 128, (y + 1) * 128)
        for h in range(2):
            blocks = [own_ref[2 * rb + h, :, cut] + other_ref[2 * rb + h, :, cut] for rb in range(4)]
            for x, block in enumerate(regroup(blocks)):
                o_buf[4 * y + x, h * jb:(h + 1) * jb, :] = block
        for x in range(NX):
            put(4 * y + x).start()
    for r in range(NR):
        put(r).wait()


def sum_pair(slots, own, other):
    block = (NR, 2 * rows_of(slots), 128)
    return pl.pallas_call(
        functools.partial(pair_kernel, slots),
        out_shape=pltpu.HBM(block, F32),
        in_specs=[VMEM] * 2,
        out_specs=HBM,
        scratch_shapes=[pltpu.VMEM(block, F32), pltpu.SemaphoreType.DMA((NR,))],
        compiler_params=pltpu.CompilerParams(vmem_limit_bytes=8 << 20),
        name="sum_pair",
    )(own, other)


def row_kernel(slots, x_ref, o_ref):
    jb = rows_of(slots)
    total = x_ref[0]
    for s in range(1, NR):
        total = total + x_ref[s]
    zero = jnp.zeros((128 - jb, 128), F32)
    for h in range(2):
        turned = jnp.concatenate([total[h * jb:(h + 1) * jb, :], zero], axis=0).T
        for rb in range(4):
            o_ref[2 * rb + h] = turned[rb * 32:(rb + 1) * 32, :]


def sum_row(slots, x):
    return pl.pallas_call(
        functools.partial(row_kernel, slots),
        out_shape=jax.ShapeDtypeStruct((NZ, PD, 128), F32),
        in_specs=[VMEM],
        out_specs=VMEM,
        compiler_params=pltpu.CompilerParams(vmem_limit_bytes=8 << 20),
        name="sum_row",
    )(x)


def last_kernel(slots, virt_ref, x_ref, sym_ref, lab_ref, o_ref):
    total = x_ref[0]
    for s in range(1, NZ):
        total = total + x_ref[s]
    for a in range(SLAB):
        at = slab_slot(virt_ref, jnp.int32(a)) if slots < SLAB else jnp.int32(a)
        x = pltpu.roll(total, lax.rem(128 - 36 * at, 128), 1) if slots > 1 else total
        keep = jnp.bitwise_xor(lab_ref[...], virt_ref[a]) == sym_ref[:, 0:36]
        o_ref[a] = jnp.where(keep, x[:, 0:36], 0.0)


def sum_last(slots, virt, x, sym, lab):
    return pl.pallas_call(
        functools.partial(last_kernel, slots),
        out_shape=jax.ShapeDtypeStruct((SLAB, PD, 36), F32),
        in_specs=[SMEM] + [VMEM] * 3,
        out_specs=VMEM,
        name="sum_last",
    )(virt, x, sym, lab)


def ladder(tiles, slots, amps_t, v_t, virt, virt_row, sym, dslots, at):
    labels_c = lax.dynamic_slice_in_dim(virt, at[0] * C, C)
    labels_d = lax.dynamic_slice_in_dim(virt, at[1] * D, D)
    cl = jnp.broadcast_to(jnp.pad(labels_c, (0, CP - C))[:, None], (CP, 128))
    bl = jnp.broadcast_to(virt[:, None], (NV, 128))
    local_sym = lax.dynamic_slice_in_dim(sym[0], at[0] * PD, PD)
    local_sym = jnp.broadcast_to(local_sym[:, None], (PD, 128))

    sent = pack_amplitudes(tiles, at, virt, dslots, amps_t, virt_row, sym)
    recv = lax.all_to_all(sent, ("y", "x"), 0, 0, tiled=True)
    vh, vl = split_integrals(v_t)
    own, away = products(slots, at, virt, dslots, recv, sym, cl, bl, vh, vl)
    other = lax.ppermute(away, "core", [(0, 1), (1, 0)])
    by_row = lax.all_to_all(sum_pair(slots, own, other), ("y", "x"), 0, 0, tiled=True)
    by_z = lax.all_to_all(sum_row(slots, by_row), "z", 0, 0, tiled=True)
    return sum_last(slots, virt, by_z, local_sym, labels_d.reshape(1, D))


def per_device(amplitudes, integrals, virt_irrep, occ_irrep, pair_index):
    row_at = lax.axis_index("y") * NX + lax.axis_index("x")
    core_at = lax.axis_index("core")
    at = jnp.stack([row_at, lax.axis_index("z") * 2 + core_at, core_at]).astype(I32)
    amps_t = jnp.transpose(amplitudes, (2, 0, 1))
    v_t = jnp.transpose(integrals, (0, 2, 1, 3))
    virt_row = virt_irrep.reshape(1, NV)
    sym, dslots, which = label_all(occ_irrep, virt_irrep, pair_index.T, virt_row)
    programs = [functools.partial(ladder, tiles, slots) for tiles, slots in FITS]
    out = lax.switch(which[0], programs, amps_t, v_t, virt_irrep, virt_row, sym, dslots, at)
    return jnp.transpose(out, (1, 0, 2))


def solution(mesh):
    fine = Mesh(mesh.devices.reshape(NY, NX, NZ, 2), ("y", "x", "z", "core"))
    rows, cols = ("y", "x"), ("z", "core")
    return jax.shard_map(
        per_device,
        mesh=fine,
        in_specs=(P(rows, None, cols), P(rows, cols, None, None), P(), P(), P()),
        out_specs=P(rows, None, cols),
        check_vma=False,
    )
```

time: 367 us -> 96.9 us (0.26)
  waiting for transfers between devices: 199 us -> 23.5 us
  local copies, waits for them, and re-layouts: 105 us -> 2.88 us
  Pallas kernels: 0 us -> 33.8 us
  matrix products: 20.2 us -> 0 us
  blocking collectives: 0 us -> 19.1 us
  other arithmetic: 19 us -> 0.08 us
  between operations: 14.2 us -> 0.68 us
  starting transfers between devices: 7.74 us -> 16.1 us
    unnamed x4 -> x0, waiting for transfers between devices: 199 us -> none
    unnamed x18 -> x2, local copies, waits for them, and re-layouts: 56.4 us -> 0.61 us
    pallas_call x0 -> x7, Pallas kernels: none -> 33.8 us  [the longest x1 12.3 us: products(): pl.pallas_call(functools.partial(products_kernel, slots), out_shape=[bloc...]
    all_to_all x1 -> x2, waiting for transfers between devices: 0.01 us -> 21.5 us  [the longest x1 12.4 us: ladder(): recv = lax.all_to_all(sent, ('y', 'x'), 0, 0, tiled=True)]
    dot_general x1 -> x0, matrix products: 20.2 us -> none  [per_device(): jnp.dot(amp_sym.reshape(pair_count, c_rows * d_cols), integrals.reshape(c...]
    all_to_all x0 -> x1, blocking collectives: none -> 19.1 us  [ladder(): lax.all_to_all(sum_pair(slots, own, other), ('y', 'x'), 0, 0, tiled=True)]
    reshape x1 -> x2, local copies, waits for them, and re-layouts: 16.2 us -> 1.3 us  [the longest x1 0.69 us: per_device(): virt_row = virt_irrep.reshape(1, NV)]
    all_to_all x2 -> x0, local copies, waits for them, and re-layouts: 12.3 us -> none  [per_device(): lax.all_to_all(amplitudes, 'row', split_axis=1, concat_axis=0, tiled=True)]
  transfers between devices with their start and end apart: 3 -> 3, of which waited for: 2 -> 3; matrix products, arithmetic and copies ran while one was open for 12% -> 1% of each run, Pallas kernels for 0% -> 11%
where the time goes in v1:
time: 96.9 us; the launch traced here: 96.4 us
  Pallas kernels  33.8 us (35%)
  waiting for transfers between devices  23.5 us (24%)
  blocking collectives  19.1 us (20%)
  starting transfers between devices  16.1 us (17%)
  local copies, waits for them, and re-layouts  2.88 us (3%)
    all_to_all x1, blocking collectives, ladder(): lax.all_to_all(sum_pair(slots, own, other), ('y', 'x'), 0, 0, tiled=True)  19.1 us
    all_to_all x1, waiting for transfers between devices, ladder(): recv = lax.all_to_all(sent, ('y', 'x'), 0, 0, tiled=True)  12.4 us
    pallas_call x1, Pallas kernels, products(): pl.pallas_call(functools.partial(products_kernel, slots), out_shape=[bloc...  12.3 us
    pallas_call x1, Pallas kernels, split_integrals(): pl.pallas_call(integrals_kernel, out_shape=[pltpu.HBM(block, BF16)] * 2,...  10.5 us
    all_to_all x1, waiting for transfers between devices, ladder(): by_z = lax.all_to_all(sum_row(slots, by_row), 'z', 0, 0, tiled=True)  9.01 us
    all_to_all x1, starting transfers between devices, ladder(): by_z = lax.all_to_all(sum_row(slots, by_row), 'z', 0, 0, tiled=True)  8.47 us
    all_to_all x1, starting transfers between devices, ladder(): recv = lax.all_to_all(sent, ('y', 'x'), 0, 0, tiled=True)  7.49 us
    pallas_call x1, Pallas kernels, pack_amplitudes(): pl.pallas_call(functools.partial(pack_kernel, tiles), out_shape=pltpu.HBM...  4.8 us
  transfers between devices with their start and end apart: 3, of which 3 were waited for; matrix products, arithmetic and copies ran while one was open for 1% of the time, Pallas kernels for 11%

profile of v1, /device:TPU:2, one launch (start us, length us, event | category | flops | bytes accessed | tf_op | source)
XLA Modules:
  0.0 96.4 jit_solution(15747684080370721570)
XLA Ops:
  0.0 0.1 pad_add_fusion
  0.1 0.7 reshape.30.row_ref
  0.8 3.1 %label_all.1 = (s32[1,512]{1,0:T(1,128)S(1)}, s32[1,576]{1,0:T(1,128)S(1)}, s32[1]{0:T(128)}) custom-call(s32[60]{0:T(128)} %occ_ref.1, s32[576]{0:T(1024)} %virt_ref.1, s32[2,512]{1,0:T(2,128)} %bitcast.26, s32[1,576]{1,0:T(1,128)S(1)} %reshape.30.row_ref), custom_call_target="tpu_custom_call" | custom-call | tf_op jit(solution)/shard_map/label_all/pallas_call | solution.py:71
  4.5 91.3 %conditional.1 = (f32[3,32,36]{2,1,0:T(8,128)S(1)}) conditional(s32[]{:T(128)} %bitcast.7, (s32[3]{0:T(128)S(1)}, s32[576]{0:T(1024)}, s32[1,576]{1,0:T(1,128)S(1)}, f32[36,32,576]{2,1,0:T(8,128)}, s32[1,576]{1,0:T(1,128)S(1)}, /*index=5*/s32[1,512]{1,0:T(1,128)S(1)}, s32[]{:T(128)}, f32[36,3,36,576]{3,2,1,0:T(8,128)}, ...), branch_computations={%region_0.1_spmd, %region_1.2_spmd, %region_2.3_spmd} | conditional | flops 8173727232 | bytes 66300752 | solution.py:406
  4.5 4.8 %pack_amplitudes.3 = f32[16,216,128]{2,1,0:T(8,128)} custom-call(s32[3]{0:T(128)S(1)} %get-tuple-element.64.at_ref, s32[576]{0:T(1024)} %get-tuple-element.62.virt_ref, s32[1,576]{1,0:T(1,128)S(1)} %get-tuple-element.65.slot_ref, f32[36,32,576]{2,1,0:T(8,128)} %get-tuple-element.66.x_hbm, s32[1,576]{1,0:T(1,128)S(1)} %get-tuple-element.67.cl_ref, ...), custom_call_target="tpu_custom_call" | custom-call | tf_op jit(solution)/shard_map/cond/branch_0_fun/pack_amplitudes/pallas_call | solution.py:120
  9.3 0.0 copy-start
  9.3 7.5 %all-to-all-start = ((f32[16,216,128]{2,1,0:T(8,128)}), f32[16,216,128]{2,1,0:T(8,128)S(1)}, u32[]{:S(2)}, u32[]{:S(2)}) async-start(f32[16,216,128]{2,1,0:T(8,128)} %pack_amplitudes.3), calls=%async_computation | async-start | bytes 3538944 | tf_op jit(solution)/shard_map/cond/branch_0_fun/all_to_all | solution.py:388
  16.8 0.0 copy-done
  16.8 0.6 dynamic-slice_bitcast_fusion
  17.4 10.5 %split_integrals.3 = (bf16[3,1536,576]{2,1,0:T(8,128)(2,1)}, bf16[3,1536,576]{2,1,0:T(8,128)(2,1)}) custom-call(f32[36,3,36,576]{3,2,1,0:T(8,128)} %get-tuple-element.70.v_hbm), custom_call_target="tpu_custom_call" | custom-call | flops 20000000 | bytes 36000000 | tf_op jit(solution)/shard_map/cond/branch_0_fun/split_integrals/pallas_call | solution.py:179
  28.0 12.4 %all-to-all-done.r_ref = f32[16,216,128]{2,1,0:T(8,128)S(1)} async-done(((f32[16,216,128]{2,1,0:T(8,128)}), f32[16,216,128]{2,1,0:T(8,128)S(1)}, u32[]{:S(2)}, u32[]{:S(2)}) %all-to-all-start) | async-done | bytes 1769504 | tf_op jit(solution)/shard_map/cond/branch_0_fun/all_to_all | solution.py:388
  40.4 0.1 broadcast_in_dim.24.cl_ref
  40.5 0.1 broadcast_in_dim.25.bl_ref
  40.6 12.3 %products.3 = (f32[8,40,512]{2,1,0:T(8,128)S(1)}, f32[8,40,512]{2,1,0:T(8,128)S(1)}) custom-call(s32[3]{0:T(128)S(1)} %get-tuple-element.64.at_ref, s32[576]{0:T(1024)S(1)} %copy-done, s32[1,576]{1,0:T(1,128)S(1)} %get-tuple-element.65.slot_ref, f32[16,216,128]{2,1,0:T(8,128)S(1)} %all-to-all-done.r_ref, s32[1,512]{1,0:T(1,128)S(1)} %get-tuple-element.68.sym_ref, ...), custom_call_target="tpu_custom_call" | custom-call | flops 8153726976 | bytes 10000000 | tf_op jit(solution)/shard_map/cond/branch_0_fun/products/pallas_call | solution.py:284
  52.9 0.1 collective-permute-start
  53.0 2.1 %collective-permute-done.other_ref = f32[8,40,512]{2,1,0:T(8,128)S(1)} collective-permute-done((f32[8,40,512]{2,1,0:T(8,128)S(1)}, f32[8,40,512]{2,1,0:T(8,128)S(1)}, u32[]{:S(2)}, u32[]{:S(2)}) %collective-permute-start) | collective-permute-done | bytes 655392 | tf_op jit(solution)/shard_map/cond/branch_0_fun/ppermute | solution.py:391
  55.1 1.4 %sum_pair.3 = f32[16,80,128]{2,1,0:T(8,128)} custom-call(f32[8,40,512]{2,1,0:T(8,128)S(1)} %get-tuple-element.73.own_ref, f32[8,40,512]{2,1,0:T(8,128)S(1)} %collective-permute-done.other_ref), custom_call_target="tpu_custom_call" | custom-call | tf_op jit(solution)/shard_map/cond/branch_0_fun/sum_pair/pallas_call | solution.py:324
  56.5 19.1 %all_to_all.36.x_ref = f32[16,80,128]{2,1,0:T(8,128)S(1)} all-to-all(f32[16,80,128]{2,1,0:T(8,128)} %sum_pair.3), channel_id=1, replica_groups=mesh['y'=4,'x'=4,'z'=8,'core'=2] {'y','x'}, dimensions={0} | all-to-all | bytes 1310720 | tf_op jit(solution)/shard_map/cond/branch_0_fun/all_to_all | solution.py:392
  75.6 0.8 sum_row.3
  76.3 8.5 %all-to-all-start.2 = ((f32[8,32,128]{2,1,0:T(8,128)}), f32[8,32,128]{2,1,0:T(8,128)S(1)}, u32[]{:S(2)}, u32[]{:S(2)}) async-start(f32[8,32,128]{2,1,0:T(8,128)} %sum_row.3), calls=%async_computation.2 | async-start | bytes 262144 | tf_op jit(solution)/shard_map/cond/branch_0_fun/all_to_all | solution.py:393
  84.8 0.1 dynamic-slice_bitcast_fusion.1
  84.9 9.0 %all-to-all-done.2.x_ref = f32[8,32,128]{2,1,0:T(8,128)S(1)} async-done(((f32[8,32,128]{2,1,0:T(8,128)}), f32[8,32,128]{2,1,0:T(8,128)S(1)}, u32[]{:S(2)}, u32[]{:S(2)}) %all-to-all-start.2) | async-done | bytes 131104 | tf_op jit(solution)/shard_map/cond/branch_0_fun/all_to_all | solution.py:393
  93.9 0.0 copy-start.3
  93.9 0.7 broadcast_in_dim.27.sym_ref
  94.6 0.0 copy-done.3
  94.6 0.9 sum_last.3
  95.8 0.0 copy-start.6
  95.8 0.6 copy-done.6
  (1 shorter events, 0.0 us)
Async XLA Ops:
  9.3 7.5 %copy-start = (s32[576]{0:T(1024)S(1)}, s32[576]{0:T(1024)}, u32[]{:S(2)}) copy-start(s32[576]{0:T(1024)} %get-tuple-element.62.virt_ref) | copy-start | bytes 6916 | tf_op jit(solution)/shard_map/cond
  9.3 31.1 %all-to-all-start = ((f32[16,216,128]{2,1,0:T(8,128)}), f32[16,216,128]{2,1,0:T(8,128)S(1)}, u32[]{:S(2)}, u32[]{:S(2)}) async-start(f32[16,216,128]{2,1,0:T(8,128)} %pack_amplitudes.3), calls=%async_computation | async-start | bytes 3538944 | tf_op jit(solution)/shard_map/cond/branch_0_fun/all_to_all | solution.py:388
  52.9 2.2 %collective-permute-start = (f32[8,40,512]{2,1,0:T(8,128)S(1)}, f32[8,40,512]{2,1,0:T(8,128)S(1)}, u32[]{:S(2)}, u32[]{:S(2)}) collective-permute-start(f32[8,40,512]{2,1,0:T(8,128)S(1)} %get-tuple-element.74), channel_id=1, source_target_pairs={{0,1},{1,0},{2,3},{3,2},{4,5},{5,4},{6,7},{7,6},{8,9},{9,8},{10,11... | collective-permute-start | bytes 1966088 | tf_op jit(solution)/shard_map/cond/branch_0_fun/ppermute | solution.py:391
  76.3 17.6 %all-to-all-start.2 = ((f32[8,32,128]{2,1,0:T(8,128)}), f32[8,32,128]{2,1,0:T(8,128)S(1)}, u32[]{:S(2)}, u32[]{:S(2)}) async-start(f32[8,32,128]{2,1,0:T(8,128)} %sum_row.3), calls=%async_computation.2 | async-start | bytes 262144 | tf_op jit(solution)/shard_map/cond/branch_0_fun/all_to_all | solution.py:393
  93.9 0.7 copy-start.3
  95.8 0.6 copy-start.6

commit v2 on v1

--- a/solution.py
+++ b/solution.py
@@ -24,7 +24,7 @@
 CP = 40
 K = D * CP
 KP = 1536
-FITS = ((6, 1), (6, 2), (9, 3))
+FITS = ((5, 1), (5, 2), (6, 2), (9, 3))
 
 SMEM = pl.BlockSpec(memory_space=pltpu.SMEM)
 VMEM = pl.BlockSpec(memory_space=pltpu.VMEM)
@@ -46,19 +46,20 @@
         found = jnp.where(pairs == o, occ_ref[o], found)
     sym_ref[...] = jnp.bitwise_xor(found[0:1], found[1:2])
 
-    labels = row_ref[...]
-    at = lax.rem(lax.broadcasted_iota(I32, labels.shape, 1), D)
+    labels = jnp.concatenate([row_ref[...], row_ref[:, 0:64]], axis=1)
+    lane = lax.broadcasted_iota(I32, labels.shape, 1)
+    at = lax.rem(lane, D)
     place = jnp.zeros_like(labels)
     for k in range(1, D):
-        same = (pltpu.roll(labels, k, 1) == labels) & (at >= k)
-        place = place + same.astype(I32)
-    top = jnp.max(place)
+        same = pltpu.roll(labels, k, 1) == labels
+        place = place + (same & (at >= k)).astype(I32)
+    top = jnp.max(jnp.where(lane < NV, place, 0))
     deep = jnp.maximum(slab_slot(virt_ref, jnp.int32(1)), slab_slot(virt_ref, jnp.int32(2)))
     which = jnp.int32(len(FITS) - 1)
     for i, (tiles, slots) in reversed(list(enumerate(FITS[:-1]))):
         which = jnp.where((top < 4 * tiles) & (deep < slots), i, which)
     which_ref[0] = which
-    slot_ref[...] = jnp.where(which < len(FITS) - 1, place, at)
+    slot_ref[...] = jnp.where(which < len(FITS) - 1, place, at)[:, 0:NV]
 
 
 def slab_slot(virt_ref, a):
@@ -81,6 +82,12 @@
     )(occ_irrep, virt_irrep, pairs, virt_row)
 
 
+def own_column(at_ref, sym_ref):
+    pair = at_ref[0] * PD + lax.broadcasted_iota(I32, (PD, PAIRS), 0)
+    mine = lax.broadcasted_iota(I32, (PD, PAIRS), 1) == pair
+    return jnp.sum(jnp.where(mine, sym_ref[...], 0), axis=1, keepdims=True)
+
+
 def pack_kernel(tiles, at_ref, virt_ref, slot_ref, x_hbm, cl_ref, sym_ref, o_hbm, x_buf, f_buf, t_buf, o_buf, in_sems, out_sems):
     def fetch(q):
         return pltpu.make_async_copy(x_hbm.at[pl.ds(4 * q, 4)], x_buf.at[pl.ds(4 * q, 4)], in_sems.at[q])
@@ -88,9 +95,7 @@
     for q in range(D // 4):
         fetch(q).start()
     f_buf[...] = jnp.zeros_like(f_buf)
-    pair = at_ref[0] * PD + lax.broadcasted_iota(I32, (PD, PAIRS), 0)
-    mine = lax.broadcasted_iota(I32, (PD, PAIRS), 1) == pair
-    sym = jnp.sum(jnp.where(mine, sym_ref[...], 0), axis=1, keepdims=True)
+    sym = own_column(at_ref, sym_ref)
     first = at_ref[1] * D
 
     @pl.loop(0, D // 4)
@@ -355,34 +360,36 @@
     )(x)
 
 
-def last_kernel(slots, virt_ref, x_ref, sym_ref, lab_ref, o_ref):
+def last_kernel(slots, at_ref, virt_ref, x_ref, sym_ref, lab_ref, o_ref):
     total = x_ref[0]
     for s in range(1, NZ):
         total = total + x_ref[s]
+    sym = own_column(at_ref, sym_ref)
     for a in range(SLAB):
-        at = slab_slot(virt_ref, jnp.int32(a)) if slots < SLAB else jnp.int32(a)
-        x = pltpu.roll(total, lax.rem(128 - 36 * at, 128), 1) if slots > 1 else total
-        keep = jnp.bitwise_xor(lab_ref[...], virt_ref[a]) == sym_ref[:, 0:36]
-        o_ref[a] = jnp.where(keep, x[:, 0:36], 0.0)
-
-
-def sum_last(slots, virt, x, sym, lab):
+        at = slab_slot(virt_ref, jnp.int32(a)) if slots < SLAB else a
+        x = total[:, 0:36]
+        for t in range(1, slots):
+            x = jnp.where(at == t, total[:, t * 36:(t + 1) * 36], x)
+        keep = jnp.bitwise_xor(lab_ref[...], virt_ref[a]) == sym
+        o_ref[a] = jnp.where(keep, x, 0.0)
+
+
+def sum_last(slots, at, virt, x, sym, lab):
     return pl.pallas_call(
         functools.partial(last_kernel, slots),
         out_shape=jax.ShapeDtypeStruct((SLAB, PD, 36), F32),
-        in_specs=[SMEM] + [VMEM] * 3,
+        in_specs=[SMEM] * 2 + [VMEM] * 3,
         out_specs=VMEM,
+        compiler_params=pltpu.CompilerParams(vmem_limit_bytes=8 << 20),
         name="sum_last",
-    )(virt, x, sym, lab)
+    )(at, virt, x, sym, lab)
 
 
 def ladder(tiles, slots, amps_t, v_t, virt, virt_row, sym, dslots, at):
     labels_c = lax.dynamic_slice_in_dim(virt, at[0] * C, C)
-    labels_d = lax.dynamic_slice_in_dim(virt, at[1] * D, D)
+    lab = lax.dynamic_slice_in_dim(virt, at[1] * D, D).reshape(1, D)
     cl = jnp.broadcast_to(jnp.pad(labels_c, (0, CP - C))[:, None], (CP, 128))
     bl = jnp.broadcast_to(virt[:, None], (NV, 128))
-    local_sym = lax.dynamic_slice_in_dim(sym[0], at[0] * PD, PD)
-    local_sym = jnp.broadcast_to(local_sym[:, None], (PD, 128))
 
     sent = pack_amplitudes(tiles, at, virt, dslots, amps_t, virt_row, sym)
     recv = lax.all_to_all(sent, ("y", "x"), 0, 0, tiled=True)
@@ -391,7 +398,7 @@
     other = lax.ppermute(away, "core", [(0, 1), (1, 0)])
     by_row = lax.all_to_all(sum_pair(slots, own, other), ("y", "x"), 0, 0, tiled=True)
     by_z = lax.all_to_all(sum_row(slots, by_row), "z", 0, 0, tiled=True)
-    return sum_last(slots, virt, by_z, local_sym, labels_d.reshape(1, D))
+    return sum_last(slots, at, virt, by_z, sym, lab)
 
 
 def per_device(amplitudes, integrals, virt_irrep, occ_irrep, pair_index):

time: 96.9 us -> 90.1 us (0.930)
  blocking collectives: 19.1 us -> 35.9 us
  waiting for transfers between devices: 23.5 us -> 12.3 us
  starting transfers between devices: 16.1 us -> 7.58 us
  Pallas kernels: 33.8 us -> 31.1 us
  local copies, waits for them, and re-layouts: 2.88 us -> 1.6 us
    all_to_all x0 -> x1, blocking collectives: none -> 17.3 us  [ladder(): by_z = lax.all_to_all(sum_row(slots, by_row), 'z', 0, 0, tiled=True)]
    all_to_all x1 -> x0, waiting for transfers between devices: 9.01 us -> none  [ladder(): by_z = lax.all_to_all(sum_row(slots, by_row), 'z', 0, 0, tiled=True)]
    all_to_all x1 -> x0, starting transfers between devices: 8.47 us -> none  [ladder(): by_z = lax.all_to_all(sum_row(slots, by_row), 'z', 0, 0, tiled=True)]
    all_to_all x1, waiting for transfers between devices: 12.4 us -> 10.2 us  [ladder(): recv = lax.all_to_all(sent, ('y', 'x'), 0, 0, tiled=True)]
    pallas_call x1, Pallas kernels: 3.07 us -> 1.69 us  [label_all(): pl.pallas_call(labels_kernel, out_shape=[jax.ShapeDtypeStruct((1, PAIRS),...]
  transfers between devices with their start and end apart: 3 -> 2, of which waited for: 3 -> 2; matrix products, arithmetic and copies ran while one was open for 1% -> 0% of each run, Pallas kernels for 11% -> 12%
where the time goes in v2:
time: 90.1 us; the launch traced here: 89.7 us
  blocking collectives  35.9 us (40%)
  Pallas kernels  31.1 us (35%)
  waiting for transfers between devices  12.3 us (14%)
  starting transfers between devices  7.58 us (8%)
  local copies, waits for them, and re-layouts  1.6 us (2%)
    all_to_all x1, blocking collectives, ladder(): lax.all_to_all(sum_pair(slots, own, other), ('y', 'x'), 0, 0, tiled=True)  18.5 us
    all_to_all x1, blocking collectives, ladder(): by_z = lax.all_to_all(sum_row(slots, by_row), 'z', 0, 0, tiled=True)  17.3 us
    pallas_call x1, Pallas kernels, products(): pl.pallas_call(functools.partial(products_kernel, slots), out_shape=[bloc...  12 us
    pallas_call x1, Pallas kernels, split_integrals(): pl.pallas_call(integrals_kernel, out_shape=[pltpu.HBM(block, BF16)] * 2,...  10.5 us
    all_to_all x1, waiting for transfers between devices, ladder(): recv = lax.all_to_all(sent, ('y', 'x'), 0, 0, tiled=True)  10.2 us
    all_to_all x1, starting transfers between devices, ladder(): recv = lax.all_to_all(sent, ('y', 'x'), 0, 0, tiled=True)  7.49 us
    pallas_call x1, Pallas kernels, pack_amplitudes(): pl.pallas_call(functools.partial(pack_kernel, tiles), out_shape=pltpu.HBM...  4.63 us
    ppermute x1, waiting for transfers between devices, ladder(): other = lax.ppermute(away, 'core', [(0, 1), (1, 0)])  2.08 us
  transfers between devices with their start and end apart: 2, of which 2 were waited for; matrix products, arithmetic and copies ran while one was open for 0% of the time, Pallas kernels for 12%

profile of v2, /device:TPU:2, one launch (start us, length us, event | category | flops | bytes accessed | tf_op | source)
XLA Modules:
  0.0 89.7 jit_solution(18426691740536470891)
XLA Ops:
  0.0 0.1 pad_add_fusion
  0.1 0.7 reshape.26.row_ref
  0.8 1.7 %label_all.1 = (s32[1,512]{1,0:T(1,128)S(1)}, s32[1,576]{1,0:T(1,128)S(1)}, s32[1]{0:T(128)}) custom-call(s32[60]{0:T(128)} %occ_ref.1, s32[576]{0:T(1024)} %virt_ref.1, s32[2,512]{1,0:T(2,128)} %bitcast.24, s32[1,576]{1,0:T(1,128)S(1)} %reshape.26.row_ref), custom_call_target="tpu_custom_call" | custom-call | tf_op jit(solution)/shard_map/label_all/pallas_call | solution.py:72
  3.1 85.9 %conditional.1 = (f32[3,32,36]{2,1,0:T(8,128)S(1)}) conditional(s32[]{:T(128)} %bitcast.5, (s32[3]{0:T(128)S(1)}, s32[576]{0:T(1024)}, s32[1,576]{1,0:T(1,128)S(1)}, f32[36,32,576]{2,1,0:T(8,128)}, s32[1,576]{1,0:T(1,128)S(1)}, /*index=5*/s32[1,512]{1,0:T(1,128)S(1)}, s32[]{:T(128)}, f32[36,3,36,576]{3,2,1,0:T(8,128)}, ...), branch_computations={%region_0.1_spmd, %region_1.2_spmd, %region_2.3_spmd, %region_3.4_... | conditional | flops 8173727232 | bytes 65628516 | solution.py:413
  3.1 4.6 %pack_amplitudes.4 = f32[16,180,128]{2,1,0:T(8,128)} custom-call(s32[3]{0:T(128)S(1)} %get-tuple-element.80.at_ref, s32[576]{0:T(1024)} %get-tuple-element.82.virt_ref, s32[1,576]{1,0:T(1,128)S(1)} %get-tuple-element.84.slot_ref, f32[36,32,576]{2,1,0:T(8,128)} %get-tuple-element.85.x_hbm, s32[1,576]{1,0:T(1,128)S(1)} %get-tuple-element.86.cl_ref, ...), custom_call_target="tpu_custom_call" | custom-call | tf_op jit(solution)/shard_map/cond/branch_0_fun/pack_amplitudes/pallas_call | solution.py:125
  7.8 0.0 copy-start
  7.8 7.5 %all-to-all-start = ((f32[16,180,128]{2,1,0:T(8,128)}), f32[16,180,128]{2,1,0:T(8,128)S(1)}, u32[]{:S(2)}, u32[]{:S(2)}) async-start(f32[16,180,128]{2,1,0:T(8,128)} %pack_amplitudes.4), calls=%async_computation | async-start | bytes 3014656 | tf_op jit(solution)/shard_map/cond/branch_0_fun/all_to_all | solution.py:395
  15.3 0.0 copy-done
  15.3 0.1 dynamic-slice_bitcast_fusion
  15.4 10.5 %split_integrals.4 = (bf16[3,1536,576]{2,1,0:T(8,128)(2,1)}, bf16[3,1536,576]{2,1,0:T(8,128)(2,1)}) custom-call(f32[36,3,36,576]{3,2,1,0:T(8,128)} %get-tuple-element.89.v_hbm), custom_call_target="tpu_custom_call" | custom-call | flops 20000000 | bytes 36000000 | tf_op jit(solution)/shard_map/cond/branch_0_fun/split_integrals/pallas_call | solution.py:184
  25.9 10.2 %all-to-all-done.r_ref = f32[16,180,128]{2,1,0:T(8,128)S(1)} async-done(((f32[16,180,128]{2,1,0:T(8,128)}), f32[16,180,128]{2,1,0:T(8,128)S(1)}, u32[]{:S(2)}, u32[]{:S(2)}) %all-to-all-start) | async-done | bytes 1474592 | tf_op jit(solution)/shard_map/cond/branch_0_fun/all_to_all | solution.py:395
  36.1 0.1 broadcast_in_dim.16.cl_ref
  36.2 0.1 broadcast_in_dim.17.bl_ref
  36.3 12.0 %products.4 = (f32[8,40,512]{2,1,0:T(8,128)S(1)}, f32[8,40,512]{2,1,0:T(8,128)S(1)}) custom-call(s32[3]{0:T(128)S(1)} %get-tuple-element.80.at_ref, s32[576]{0:T(1024)S(1)} %copy-done, s32[1,576]{1,0:T(1,128)S(1)} %get-tuple-element.84.slot_ref, f32[16,180,128]{2,1,0:T(8,128)S(1)} %all-to-all-done.r_ref, s32[1,512]{1,0:T(1,128)S(1)} %get-tuple-element.87.sym_ref, ...), custom_call_target="tpu_custom_call" | custom-call | flops 8153726976 | bytes 10000000 | tf_op jit(solution)/shard_map/cond/branch_0_fun/products/pallas_call | solution.py:289
  48.3 0.1 collective-permute-start
  48.4 2.1 %collective-permute-done.other_ref = f32[8,40,512]{2,1,0:T(8,128)S(1)} collective-permute-done((f32[8,40,512]{2,1,0:T(8,128)S(1)}, f32[8,40,512]{2,1,0:T(8,128)S(1)}, u32[]{:S(2)}, u32[]{:S(2)}) %collective-permute-start) | collective-permute-done | bytes 655392 | tf_op jit(solution)/shard_map/cond/branch_0_fun/ppermute | solution.py:398
  50.5 1.4 %sum_pair.4 = f32[16,80,128]{2,1,0:T(8,128)} custom-call(f32[8,40,512]{2,1,0:T(8,128)S(1)} %get-tuple-element.92.own_ref, f32[8,40,512]{2,1,0:T(8,128)S(1)} %collective-permute-done.other_ref), custom_call_target="tpu_custom_call" | custom-call | tf_op jit(solution)/shard_map/cond/branch_0_fun/sum_pair/pallas_call | solution.py:329
  51.9 18.5 %all_to_all.48.x_ref = f32[16,80,128]{2,1,0:T(8,128)S(1)} all-to-all(f32[16,80,128]{2,1,0:T(8,128)} %sum_pair.4), channel_id=1, replica_groups=mesh['y'=4,'x'=4,'z'=8,'core'=2] {'y','x'}, dimensions={0} | all-to-all | bytes 1310720 | tf_op jit(solution)/shard_map/cond/branch_0_fun/all_to_all | solution.py:399
  70.5 0.1 sum_row.4
  70.6 17.3 %all_to_all.49.x_ref = f32[8,32,128]{2,1,0:T(8,128)S(1)} all-to-all(f32[8,32,128]{2,1,0:T(8,128)S(1)} %sum_row.4), channel_id=1, replica_groups=mesh['y'=4,'x'=4,'z'=8,'core'=2] {'z'}, dimensions={0} | all-to-all | bytes 262144 | tf_op jit(solution)/shard_map/cond/branch_0_fun/all_to_all | solution.py:400
  87.9 0.7 sum_last.4
  89.1 0.0 copy-start.4
  89.1 0.6 copy-done.4
  (1 shorter events, 0.0 us)
Async XLA Ops:
  7.8 7.5 %copy-start = (s32[576]{0:T(1024)S(1)}, s32[576]{0:T(1024)}, u32[]{:S(2)}) copy-start(s32[576]{0:T(1024)} %get-tuple-element.82.virt_ref) | copy-start | bytes 6916 | tf_op jit(solution)/shard_map/cond
  7.8 28.3 %all-to-all-start = ((f32[16,180,128]{2,1,0:T(8,128)}), f32[16,180,128]{2,1,0:T(8,128)S(1)}, u32[]{:S(2)}, u32[]{:S(2)}) async-start(f32[16,180,128]{2,1,0:T(8,128)} %pack_amplitudes.4), calls=%async_computation | async-start | bytes 3014656 | tf_op jit(solution)/shard_map/cond/branch_0_fun/all_to_all | solution.py:395
  48.3 2.2 %collective-permute-start = (f32[8,40,512]{2,1,0:T(8,128)S(1)}, f32[8,40,512]{2,1,0:T(8,128)S(1)}, u32[]{:S(2)}, u32[]{:S(2)}) collective-permute-start(f32[8,40,512]{2,1,0:T(8,128)S(1)} %get-tuple-element.93), channel_id=1, source_target_pairs={{0,1},{1,0},{2,3},{3,2},{4,5},{5,4},{6,7},{7,6},{8,9},{9,8},{10,11... | collective-permute-start | bytes 1966088 | tf_op jit(solution)/shard_map/cond/branch_0_fun/ppermute | solution.py:398
  89.1 0.6 copy-start.4
